TPU v7x, 512 devices: a whole 4x8x8 slice. The times are simulated.
512 devices in a mesh: snap: 8 (over z), tile: 64 (over x, y, core).
Axes of the slice: x: 4, y: 8, z: 8, core: 2. Of those that a mesh axis runs over, the one named last changes fastest.
Arguments:
- modes: bfloat16 [8192, 256], P(('snap', 'tile')), may hold values from -8 to 8
- targets: bfloat16 [8192, 256], P(('snap', 'tile')), may hold values from -16 to 16
- pairs: int32 [4096, 2], replicated, may hold values from 0 to 256, as said below
- support: int32 [4096, 256], P(('snap', 'tile')), may hold values from 0 to 1, as said below
Outputs:
- coeffs: float32 [4096, 256], P(('snap', 'tile'))
- resid: float32 [4096, 256], P(('snap', 'tile'))
Inputs may be any that keep to these rules, and one draw needn't show every extreme that they name: Rows are distinct unordered pairs; the first entry is below 256; every index below 256 is the first entry of exactly 16 rows. `support`: every target has at least one active term.
All inputs are finite; a program needn't handle non-finite values.
Results may differ from a plain program's by a relative error of at most 0.0036.
Values may be sent and summed in bfloat16 or wider, within the bound.
A program may use at most 64 MiB of HBM per device.

v0:
```python
import jax
import jax.numpy as jnp
from jax import lax
from jax.sharding import PartitionSpec as P

ITERS = 2


def widened(rows_in):
    return jnp.concatenate(
        [rows_in.astype(jnp.float32), jnp.ones((rows_in.shape[0], 1), jnp.float32)], axis=1
    )


def body(modes, targets, pairs, support):
    snap_count = lax.axis_size("snap")
    tile_count = lax.axis_size("tile")
    term_count = pairs.shape[0]
    mode_count = modes.shape[1]
    target_count = targets.shape[1]
    share_rows = term_count // (snap_count * tile_count)
    total_snaps = modes.shape[0] * snap_count * tile_count
    tile_at = lax.axis_index("tile")
    term_grid = jnp.arange(term_count, dtype=jnp.int32).reshape(snap_count, tile_count, share_rows)
    own_terms = lax.dynamic_index_in_dim(term_grid, tile_at, 1, keepdims=False).reshape(-1)
    first_factor = pairs[:, 0]
    second_factor = pairs[:, 1]
    start_sums = (
        jnp.zeros((snap_count * share_rows, term_count), jnp.float32),
        jnp.zeros((snap_count * share_rows, target_count), jnp.float32),
    )
    rows_in = lax.all_gather(modes, "tile", axis=0, tiled=True)
    count_rows = rows_in.shape[0]
    block_rows = max((divisor for divisor in range(1, 513) if count_rows % divisor == 0))

    def inner(totals, block_item):
        block_modes, block_targets = block_item
        extended = widened(block_modes)
        library = (
            jnp.take(extended, first_factor, axis=1) * jnp.take(extended, second_factor, axis=1)
        ).astype(jnp.bfloat16)
        mine = jnp.take(library, own_terms, axis=1)
        gram_sum = totals[0] + lax.dot_general(
            mine, library, (((0,), (0,)), ((), ())), preferred_element_type=jnp.float32
        )
        cross_sum = totals[1] + lax.dot_general(
            mine, block_targets, (((0,), (0,)), ((), ())), preferred_element_type=jnp.float32
        )
        return ((gram_sum, cross_sum), None)

    blocks = (
        rows_in.reshape(count_rows // block_rows, block_rows, mode_count),
        lax.all_gather(targets, "tile", axis=0, tiled=True).reshape(
            count_rows // block_rows, block_rows, target_count
        ),
    )
    results, _ = lax.scan(inner, start_sums, blocks)
    gram_part, cross_part = results
    gram_all, cross_all = lax.psum((gram_part, cross_part), "snap")
    snap_at = lax.axis_index("snap")
    gram_rows = lax.dynamic_slice_in_dim(gram_all, snap_at * share_rows, share_rows, 0)
    cross_rows = lax.dynamic_slice_in_dim(cross_all, snap_at * share_rows, share_rows, 0)
    gram_rows = gram_rows / total_snaps
    cross_rows = cross_rows / total_snaps
    support_mask = support.astype(jnp.float32)

    def energy_of(vector):
        return lax.psum(jnp.sum(vector * vector, axis=0), ("snap", "tile"))

    resid = support_mask * cross_rows
    coeffs = jnp.zeros_like(resid)
    direction = resid
    energy = energy_of(resid)
    for step in range(ITERS):
        product = jnp.dot(
            gram_rows,
            lax.all_gather(direction, ("snap", "tile"), axis=0, tiled=True),
            precision=lax.Precision.HIGHEST,
            preferred_element_type=jnp.float32,
        )
        image = support_mask * product
        step_len = energy / lax.psum(jnp.sum(direction * image, axis=0), ("snap", "tile"))
        coeffs = coeffs + step_len * direction
        resid = resid - step_len * image
        if step + 1 < ITERS:
            fresh = energy_of(resid)
            direction = resid + fresh / energy * direction
            energy = fresh
    return (coeffs, resid)


def solution(mesh):
    return jax.shard_map(
        body,
        mesh=mesh,
        in_specs=(
            P(("snap", "tile"), None),
            P(("snap", "tile"), None),
            P(),
            P(("snap", "tile"), None),
        ),
        out_specs=(P(("snap", "tile"), None), P(("snap", "tile"), None)),
        check_vma=False,
    )
```

profile of v0, /device:TPU:1, one launch (start us, length us, event | category | flops | bytes accessed | tf_op | source)
XLA Modules:
  0.0 834.8 jit_solution(8397565621540414149)
XLA Ops:
  7.3 0.9 fusion.16
  8.2 54.4 %all_gather.12 = bf16[1024,256]{1,0:T(8,128)(2,1)S(1)} all-gather(bf16[16,256]{1,0:T(8,128)(2,1)} %param.8), channel_id=1, replica_groups=mesh['snap'=8,'tile'=64] {'tile'}, dimensions={0}, use_global_device_ids=true | all-gather | bytes 532480 | tf_op jit(solution)/shard_map/all_gather | solution.py:32
  62.6 49.5 %all_gather.13 = bf16[1024,256]{1,0:T(8,128)(2,1)S(1)} all-gather(bf16[16,256]{1,0:T(8,128)(2,1)} %param.9), channel_id=1, replica_groups=mesh['snap'=8,'tile'=64] {'tile'}, dimensions={0}, use_global_device_ids=true | all-gather | bytes 532480 | tf_op jit(solution)/shard_map/all_gather | solution.py:53
  112.0 101.3 %while.13 = (s32[]{:T(128)}, f32[64,4096]{1,0:T(8,128)S(1)}, f32[64,256]{1,0:T(8,128)S(1)}, s32[64]{0:T(128)S(1)}, bf16[2,512,256]{2,1,0:T(8,128)(2,1)S(1)}, /*i...) while((s32[]{:T(128)}, f32[64,4096]{1,0:T(8,128)S(1)}, ...), condition=%wide.region_1.3_spmd.clone, body=%wide.region_0.2_spmd.clone.sunk | while | flops 294438976 | bytes 63463412 | solution.py:57
  112.3 16.9 %gather_fusion.1 = f32[4096,512]{1,0:T(8,128)} fusion(f32[512,257]{0,1:T(8,128)S(1)} %pad_convert_fusion.2, s32[4096]{0:T(1024)S(1)} %get-tuple-element.170), kind=kCustom, calls=%fused_computation.clone.clone.1 | custom fusion | bytes 16793600 | tf_op jit(solution)/shard_map/while/body/eval_jaxpr/jit(_take)/gather | solution.py:40
  129.2 16.9 %gather_fusion = f32[4096,512]{1,0:T(8,128)} fusion(f32[512,257]{0,1:T(8,128)S(1)} %pad_convert_fusion.2, s32[4096]{0:T(1024)S(1)} %get-tuple-element.169), kind=kCustom, calls=%fused_computation.1.clone.clone.1 | custom fusion | bytes 16793600 | tf_op jit(solution)/shard_map/while/body/eval_jaxpr/jit(_take)/gather | solution.py:40
  146.1 9.2 %fusion.28 = bf16[512,4096]{0,1:T(8,128)(2,1)} fusion(f32[4096,512]{1,0:T(8,128)} %gather_fusion, f32[4096,512]{1,0:T(8,128)} %gather_fusion.1, pred[4096]{0:T(1024)(128)(4,1)S(1)} %get-tuple-element.171, pred[4096]{0:T(1024)(128)(4,1)S(1)} %get-tuple-element.172), kind=kLoop, calls=%fused_computation.4.clone.1 | loop fusion | flops 8388608 | bytes 20979712 | tf_op jit(solution)/shard_map/while/body/eval_jaxpr/convert_element_type | solution.py:41
  155.3 3.4 gather_fusion.2
  158.8 3.7 convolution_add_fusion.4
  163.0 16.9 %gather_fusion.1 = f32[4096,512]{1,0:T(8,128)} fusion(f32[512,257]{0,1:T(8,128)S(1)} %pad_convert_fusion.2, s32[4096]{0:T(1024)S(1)} %get-tuple-element.170), kind=kCustom, calls=%fused_computation.clone.clone.1 | custom fusion | bytes 16793600 | tf_op jit(solution)/shard_map/while/body/eval_jaxpr/jit(_take)/gather | solution.py:40
  179.8 16.9 %gather_fusion = f32[4096,512]{1,0:T(8,128)} fusion(f32[512,257]{0,1:T(8,128)S(1)} %pad_convert_fusion.2, s32[4096]{0:T(1024)S(1)} %get-tuple-element.169), kind=kCustom, calls=%fused_computation.1.clone.clone.1 | custom fusion | bytes 16793600 | tf_op jit(solution)/shard_map/while/body/eval_jaxpr/jit(_take)/gather | solution.py:40
  196.7 9.2 %fusion.28 = bf16[512,4096]{0,1:T(8,128)(2,1)} fusion(f32[4096,512]{1,0:T(8,128)} %gather_fusion, f32[4096,512]{1,0:T(8,128)} %gather_fusion.1, pred[4096]{0:T(1024)(128)(4,1)S(1)} %get-tuple-element.171, pred[4096]{0:T(1024)(128)(4,1)S(1)} %get-tuple-element.172), kind=kLoop, calls=%fused_computation.4.clone.1 | loop fusion | flops 8388608 | bytes 20979712 | tf_op jit(solution)/shard_map/while/body/eval_jaxpr/convert_element_type | solution.py:41
  205.9 3.4 gather_fusion.2
  209.4 3.7 convolution_add_fusion.4
  213.4 1.0 copy-done
  214.4 77.7 %all-reduce.5.cloned.1.call-done = (f32[64,256]{1,0:T(8,128)}, f32[64,4096]{1,0:T(8,128)}) async-done(((f32[64,256]{1,0:T(8,128)}, f32[64,4096]{1,0:T(8,128)}), (f32[64,256]{1,0:T(8,128)}, f32[64,4096]{1,0:T(8,128)})) %all-reduce.5.cloned.1.call-update) | async-done | bytes 1114128 | tf_op jit(solution)/shard_map/psum | solution.py:59
  292.2 1.3 multiply_multiply_fusion
  293.5 124.9 %all-gather.3.cloned.1.call-done = f32[4096,256]{1,0:T(8,128)} async-done(((f32[8,256]{1,0:T(8,128)}), f32[4096,256]{1,0:T(8,128)}) %all-gather.3.cloned.1.call-update) | async-done | bytes 4194320 | tf_op jit(solution)/shard_map/all_gather | solution.py:77
  418.5 3.9 multiply_reduce_fusion.2
  422.4 96.1 %all-reduce.1 = (f32[256]{0:T(256)S(1)}, f32[256]{0:T(256)S(1)}) all-reduce(f32[256]{0:T(256)S(1)} %get-tuple-element.84, f32[256]{0:T(256)S(1)} %get-tuple-element.83), channel_id=1, replica_groups=mesh['snap'=8,'tile'=64] {'snap','tile'}, use_global_device_ids=true, to_apply=%region_4.6 | all-reduce | flops 512 | bytes 4096 | tf_op jit(solution)/shard_map/psum | solution.py:68
  518.6 93.8 %psum.46 = f32[256]{0:T(256)S(1)} all-reduce(f32[256]{0:T(256)S(1)} %multiply_reduce_fusion.1), channel_id=1, replica_groups=mesh['snap'=8,'tile'=64] {'snap','tile'}, use_global_device_ids=true, to_apply=%region_9.11 | all-reduce | flops 256 | bytes 2048 | tf_op jit(solution)/shard_map/psum | solution.py:68
  613.0 114.6 %all-gather.5.cloned.1.call-done = f32[4096,256]{1,0:T(8,128)} async-done(((f32[8,256]{1,0:T(8,128)}), f32[4096,256]{1,0:T(8,128)}) %all-gather.5.cloned.1.call-update) | async-done | bytes 4194320 | tf_op jit(solution)/shard_map/all_gather | solution.py:77
  727.6 3.9 multiply_reduce_fusion
  731.5 96.2 %psum.47 = f32[256]{0:T(256)S(1)} all-reduce(f32[256]{0:T(256)S(1)} %get-tuple-element.114), channel_id=1, replica_groups=mesh['snap'=8,'tile'=64] {'snap','tile'}, use_global_device_ids=true, to_apply=%region_11.13 | all-reduce | flops 256 | bytes 2048 | tf_op jit(solution)/shard_map/psum | solution.py:82
  (43 shorter events, 2.5 us)
Async XLA Ops:
  7.2 285.0 %all-reduce.5.cloned.1.call-start = ((), (), s32[]{:S(2)}) async-start(), calls=%async_computation.2 | async-start | bytes 2228224 | tf_op jit(solution)/shard_map/psum | solution.py:59
  112.0 180.1 %copy-start.4 = (s32[8,256]{1,0:T(8,128)S(1)}, s32[8,256]{1,0:T(8,128)}, u32[]{:S(2)}) copy-start(s32[8,256]{1,0:T(8,128)} %param.11) | copy-start | bytes 24580
  213.3 1.0 copy-start
  213.3 1.0 copy-start.1
  214.4 204.1 %all-gather.3.cloned.1.call-start = ((), (), s32[]{:S(2)}) async-start(), calls=%async_computation | async-start | bytes 4202496 | tf_op jit(solution)/shard_map/all_gather | solution.py:77
  293.5 225.1 %copy-start.2 = (f32[8,256]{1,0:T(8,128)S(1)}, f32[8,256]{1,0:T(8,128)}, u32[]{:S(2)}) copy-start(f32[8,256]{1,0:T(8,128)} %multiply_multiply_fusion) | copy-start | bytes 24580
  293.5 434.1 %all-gather.5.cloned.1.call-start = ((), (), s32[]{:S(2)}) async-start(), calls=%async_computation.1 | async-start | bytes 4202496 | tf_op jit(solution)/shard_map/all_gather | solution.py:77
  613.0 214.7 %copy-start.3 = (f32[8,256]{1,0:T(8,128)S(1)}, f32[8,256]{1,0:T(8,128)}, u32[]{:S(2)}) copy-start(f32[8,256]{1,0:T(8,128)} %multiply_add_fusion.1) | copy-start | bytes 24580
Sparse Core Ops, SparseCore 0:
  214.5 77.6 all-reduce.4
  297.6 120.7 all-gather.2
  613.1 114.4 all-gather.4
where the time goes:
time: 835 us
  blocking collectives  390 us (47%)
  waiting for transfers between devices  317 us (38%)
  local copies, waits for them, and re-layouts  76.7 us (9%)
  other arithmetic  21.2 us (3%)
  matrix products  15.7 us (2%)
  between operations  13.8 us (2%)
    all_gather x2, waiting for transfers between devices, body(): lax.all_gather(direction, ('snap', 'tile'), axis=0, tiled=True)  239 us
    psum x2, blocking collectives, energy_of(): return lax.psum(jnp.sum(vector * vector, axis=0), ('snap', 'tile'))  190 us
    psum x1, blocking collectives, body(): lax.psum(jnp.sum(direction * image, axis=0), ('snap', 'tile'))  96.2 us
    psum x1, waiting for transfers between devices, body(): gram_all, cross_all = lax.psum((gram_part, cross_part), 'snap')  77.7 us
    all_gather x1, blocking collectives, body(): rows_in = lax.all_gather(modes, 'tile', axis=0, tiled=True)  54.4 us
    all_gather x1, blocking collectives, body(): lax.all_gather(targets, 'tile', axis=0, tiled=True)  49.5 us
    gather x2, local copies, waits for them, and re-layouts, inner(): jnp.take(extended, first_factor, axis=1)  33.8 us
    gather x2, local copies, waits for them, and re-layouts, inner(): jnp.take(extended, second_factor, axis=1)  33.7 us
  transfers between devices with their start and end apart: 3, of which 3 were waited for; matrix products, arithmetic and copies ran while one was open for 0% of the time, Pallas kernels for 0%

commit v1 on v0

--- a/solution.py
+++ b/solution.py
@@ -1,9 +1,18 @@
+import functools
 import jax
 import jax.numpy as jnp
 from jax import lax
 from jax.sharding import PartitionSpec as P
 
 ITERS = 2
+
+
+def _unite_slices(xx, ax_name):
+    carry_in = jax.lax.all_gather(xx, ax_name)
+    return jnp.sum(carry_in, axis=0)
+
+
+screen_spread = functools.partial(_unite_slices, ax_name=("snap", "tile"))
 
 
 def widened(rows_in):
@@ -65,7 +74,7 @@
     support_mask = support.astype(jnp.float32)
 
     def energy_of(vector):
-        return lax.psum(jnp.sum(vector * vector, axis=0), ("snap", "tile"))
+        return screen_spread(jnp.sum(vector * vector, axis=0))
 
     resid = support_mask * cross_rows
     coeffs = jnp.zeros_like(resid)

time: 835 us -> 875 us (1.048)
  blocking collectives: 390 us -> 430 us
    psum x2 -> x0, blocking collectives: 190 us -> none  [energy_of(): return lax.psum(jnp.sum(vector * vector, axis=0), ('snap', 'tile'))]
    all_gather x0 -> x2, blocking collectives: none -> 134 us  [_unite_slices(): carry_in = jax.lax.all_gather(xx, ax_name)]
    psum x1 -> x2, blocking collectives: 96.2 us -> 191 us  [body(): lax.psum(jnp.sum(direction * image, axis=0), ('snap', 'tile'))]
where the time goes in v1:
time: 875 us; the launch traced here: 874 us
  blocking collectives  430 us (49%)
  waiting for transfers between devices  316 us (36%)
  local copies, waits for them, and re-layouts  76.3 us (9%)
  other arithmetic  22.3 us (3%)
  matrix products  15.7 us (2%)
  between operations  13.8 us (2%)
    all_gather x2, waiting for transfers between devices, body(): lax.all_gather(direction, ('snap', 'tile'), axis=0, tiled=True)  239 us
    psum x2, blocking collectives, body(): lax.psum(jnp.sum(direction * image, axis=0), ('snap', 'tile'))  191 us
    all_gather x2, blocking collectives, _unite_slices(): carry_in = jax.lax.all_gather(xx, ax_name)  134 us
    psum x1, waiting for transfers between devices, body(): gram_all, cross_all = lax.psum((gram_part, cross_part), 'snap')  77.7 us
    all_gather x1, blocking collectives, body(): rows_in = lax.all_gather(modes, 'tile', axis=0, tiled=True)  54.4 us
    all_gather x1, blocking collectives, body(): lax.all_gather(targets, 'tile', axis=0, tiled=True)  49.5 us
    gather x2, local copies, waits for them, and re-layouts, inner(): jnp.take(extended, first_factor, axis=1)  33.6 us
    gather x2, local copies, waits for them, and re-layouts, inner(): jnp.take(extended, second_factor, axis=1)  33.6 us
  transfers between devices with their start and end apart: 3, of which 3 were waited for; matrix products, arithmetic and copies ran while one was open for 0% of the time, Pallas kernels for 0%

profile of v1, /device:TPU:1, one launch (start us, length us, event | category | flops | bytes accessed | tf_op | source)
XLA Modules:
  0.0 874.4 jit_solution(2667893897141048627)
XLA Ops:
  8.2 54.4 %all_gather.24 = bf16[1024,256]{1,0:T(8,128)(2,1)S(1)} all-gather(bf16[16,256]{1,0:T(8,128)(2,1)} %param.8), channel_id=1, replica_groups=mesh['snap'=8,'tile'=64] {'tile'}, dimensions={0}, use_global_device_ids=true | all-gather | bytes 532480 | tf_op jit(solution)/shard_map/all_gather | solution.py:41
  62.6 49.5 %all_gather.25 = bf16[1024,256]{1,0:T(8,128)(2,1)S(1)} all-gather(bf16[16,256]{1,0:T(8,128)(2,1)} %param.9), channel_id=1, replica_groups=mesh['snap'=8,'tile'=64] {'tile'}, dimensions={0}, use_global_device_ids=true | all-gather | bytes 532480 | tf_op jit(solution)/shard_map/all_gather | solution.py:62
  112.0 101.0 %while.13 = (s32[]{:T(128)}, f32[64,4096]{1,0:T(8,128)S(1)}, f32[64,256]{1,0:T(8,128)S(1)}, s32[64]{0:T(128)S(1)}, bf16[2,512,256]{2,1,0:T(8,128)(2,1)S(1)}, /*i...) while((s32[]{:T(128)}, f32[64,4096]{1,0:T(8,128)S(1)}, ...), condition=%wide.region_1.3_spmd.clone, body=%wide.region_0.2_spmd.clone.sunk | while | flops 294438976 | bytes 63463412 | solution.py:66
  112.3 16.8 %gather_fusion.1 = f32[4096,512]{1,0:T(8,128)} fusion(f32[512,257]{0,1:T(8,128)S(1)} %pad_convert_fusion.2, s32[4096]{0:T(1024)S(1)} %get-tuple-element.176), kind=kCustom, calls=%fused_computation.clone.clone.1 | custom fusion | bytes 16793600 | tf_op jit(solution)/shard_map/while/body/eval_jaxpr/jit(_take)/gather | solution.py:49
  129.1 16.8 %gather_fusion = f32[4096,512]{1,0:T(8,128)} fusion(f32[512,257]{0,1:T(8,128)S(1)} %pad_convert_fusion.2, s32[4096]{0:T(1024)S(1)} %get-tuple-element.175), kind=kCustom, calls=%fused_computation.1.clone.clone.1 | custom fusion | bytes 16793600 | tf_op jit(solution)/shard_map/while/body/eval_jaxpr/jit(_take)/gather | solution.py:49
  145.9 9.2 %fusion.28 = bf16[512,4096]{0,1:T(8,128)(2,1)} fusion(f32[4096,512]{1,0:T(8,128)} %gather_fusion, f32[4096,512]{1,0:T(8,128)} %gather_fusion.1, pred[4096]{0:T(1024)(128)(4,1)S(1)} %get-tuple-element.177, pred[4096]{0:T(1024)(128)(4,1)S(1)} %get-tuple-element.178), kind=kLoop, calls=%fused_computation.4.clone.1 | loop fusion | flops 8388608 | bytes 20979712 | tf_op jit(solution)/shard_map/while/body/eval_jaxpr/convert_element_type | solution.py:50
  155.1 3.4 gather_fusion.2
  158.6 3.7 convolution_add_fusion.4
  162.8 16.8 %gather_fusion.1 = f32[4096,512]{1,0:T(8,128)} fusion(f32[512,257]{0,1:T(8,128)S(1)} %pad_convert_fusion.2, s32[4096]{0:T(1024)S(1)} %get-tuple-element.176), kind=kCustom, calls=%fused_computation.clone.clone.1 | custom fusion | bytes 16793600 | tf_op jit(solution)/shard_map/while/body/eval_jaxpr/jit(_take)/gather | solution.py:49
  179.6 16.8 %gather_fusion = f32[4096,512]{1,0:T(8,128)} fusion(f32[512,257]{0,1:T(8,128)S(1)} %pad_convert_fusion.2, s32[4096]{0:T(1024)S(1)} %get-tuple-element.175), kind=kCustom, calls=%fused_computation.1.clone.clone.1 | custom fusion | bytes 16793600 | tf_op jit(solution)/shard_map/while/body/eval_jaxpr/jit(_take)/gather | solution.py:49
  196.4 9.2 %fusion.28 = bf16[512,4096]{0,1:T(8,128)(2,1)} fusion(f32[4096,512]{1,0:T(8,128)} %gather_fusion, f32[4096,512]{1,0:T(8,128)} %gather_fusion.1, pred[4096]{0:T(1024)(128)(4,1)S(1)} %get-tuple-element.177, pred[4096]{0:T(1024)(128)(4,1)S(1)} %get-tuple-element.178), kind=kLoop, calls=%fused_computation.4.clone.1 | loop fusion | flops 8388608 | bytes 20979712 | tf_op jit(solution)/shard_map/while/body/eval_jaxpr/convert_element_type | solution.py:50
  205.6 3.4 gather_fusion.2
  209.1 3.7 convolution_add_fusion.4
  213.0 1.0 copy-done
  214.1 77.7 %all-reduce.4.cloned.1.call-done = (f32[64,256]{1,0:T(8,128)}, f32[64,4096]{1,0:T(8,128)}) async-done(((f32[64,256]{1,0:T(8,128)}, f32[64,4096]{1,0:T(8,128)}), (f32[64,256]{1,0:T(8,128)}, f32[64,4096]{1,0:T(8,128)})) %all-reduce.4.cloned.1.call-update) | async-done | bytes 1114128 | tf_op jit(solution)/shard_map/psum | solution.py:68
  291.8 1.3 multiply_multiply_fusion
  293.2 124.9 %all-gather.7.cloned.1.call-done = f32[4096,256]{1,0:T(8,128)} async-done(((f32[8,256]{1,0:T(8,128)}), f32[4096,256]{1,0:T(8,128)}) %all-gather.7.cloned.1.call-update) | async-done | bytes 4194320 | tf_op jit(solution)/shard_map/all_gather | solution.py:86
  418.1 3.9 multiply_reduce_fusion.2
  422.1 67.5 %all-gather.2 = f32[512,1,256]{2,1,0:T(1,128)S(1)} all-gather(f32[1,1,256]{2,1,0:T(1,128)S(1)} %bitcast.45), channel_id=2, replica_groups=mesh['snap'=8,'tile'=64] {'snap','tile'}, dimensions={0}, use_global_device_ids=true | all-gather | bytes 525312 | tf_op jit(solution)/shard_map/all_gather | solution.py:11
  489.5 95.2 %psum.30 = f32[256]{0:T(256)S(1)} all-reduce(f32[256]{0:T(256)S(1)} %get-tuple-element.91), channel_id=1, replica_groups=mesh['snap'=8,'tile'=64] {'snap','tile'}, use_global_device_ids=true, to_apply=%region_7.9 | all-reduce | flops 256 | bytes 2048 | tf_op jit(solution)/shard_map/psum | solution.py:91
  585.4 66.9 %all-gather.3 = f32[512,1,256]{2,1,0:T(1,128)S(1)} all-gather(f32[1,1,256]{2,1,0:T(1,128)S(1)} %bitcast.44), channel_id=3, replica_groups=mesh['snap'=8,'tile'=64] {'snap','tile'}, dimensions={0}, use_global_device_ids=true | all-gather | bytes 525312 | tf_op jit(solution)/shard_map/all_gather | solution.py:11
  653.4 113.7 %all-gather.9.cloned.1.call-done = f32[4096,256]{1,0:T(8,128)} async-done(((f32[8,256]{1,0:T(8,128)}), f32[4096,256]{1,0:T(8,128)}) %all-gather.9.cloned.1.call-update) | async-done | bytes 4194320 | tf_op jit(solution)/shard_map/all_gather | solution.py:86
  767.2 3.9 multiply_reduce_fusion
  771.1 96.2 %psum.31 = f32[256]{0:T(256)S(1)} all-reduce(f32[256]{0:T(256)S(1)} %get-tuple-element.120), channel_id=1, replica_groups=mesh['snap'=8,'tile'=64] {'snap','tile'}, use_global_device_ids=true, to_apply=%region_11.13 | all-reduce | flops 256 | bytes 2048 | tf_op jit(solution)/shard_map/psum | solution.py:91
  (46 shorter events, 4.5 us)
Async XLA Ops:
  7.2 284.7 %all-reduce.4.cloned.1.call-start = ((), (), s32[]{:S(2)}) async-start(), calls=%async_computation.2 | async-start | bytes 2228224 | tf_op jit(solution)/shard_map/psum | solution.py:68
  112.0 179.8 %copy-start.4 = (s32[8,256]{1,0:T(8,128)S(1)}, s32[8,256]{1,0:T(8,128)}, u32[]{:S(2)}) copy-start(s32[8,256]{1,0:T(8,128)} %param.11) | copy-start | bytes 24580
  213.0 1.0 copy-start
  213.0 1.0 copy-start.1
  214.1 204.1 %all-gather.7.cloned.1.call-start = ((), (), s32[]{:S(2)}) async-start(), calls=%async_computation | async-start | bytes 4202496 | tf_op jit(solution)/shard_map/all_gather | solution.py:86
  293.1 292.2 %copy-start.2 = (f32[8,256]{1,0:T(8,128)S(1)}, f32[8,256]{1,0:T(8,128)}, u32[]{:S(2)}) copy-start(f32[8,256]{1,0:T(8,128)} %multiply_multiply_fusion) | copy-start | bytes 24580
  293.2 474.0 %all-gather.9.cloned.1.call-start = ((), (), s32[]{:S(2)}) async-start(), calls=%async_computation.1 | async-start | bytes 4202496 | tf_op jit(solution)/shard_map/all_gather | solution.py:86
  653.4 213.8 %copy-start.3 = (f32[8,256]{1,0:T(8,128)S(1)}, f32[8,256]{1,0:T(8,128)}, u32[]{:S(2)}) copy-start(f32[8,256]{1,0:T(8,128)} %multiply_add_fusion.1) | copy-start | bytes 24580
Sparse Core Ops, SparseCore 0:
  214.2 77.6 all-reduce.3
  297.3 120.7 all-gather.6
  653.6 113.5 all-gather.8
